TPU v7x, 32 devices: a whole 2x2x4 slice. The times are simulated.
32 devices in a mesh: dp: 8 (over y, x, core), seq: 4 (over z).
Axes of the slice: x: 2, y: 2, z: 4, core: 2. Of those that a mesh axis runs over, the one named last changes fastest.
Arguments:
- tokens: bfloat16 [16, 2048, 960], P('dp', 'seq'), may hold values from -6 to 6
- segments: int32 [16, 2048], P('dp'), may hold values from 0 to 2047, as said below
- cotangent: bfloat16 [16, 2048, 960], P('dp', 'seq'), may hold values from -6 to 6
- attn_gain: bfloat16 [960], replicated, may hold values from 0.099609375 to 1.8984375
- mlp_gain: bfloat16 [960], replicated, may hold values from 0.099609375 to 1.8984375
- query_key_value_weight: bfloat16 [1536000], P(('dp', 'seq')), may hold values from -0.1875 to 0.1875
- w_out: bfloat16 [921600], P(('dp', 'seq')), may hold values from -1.5 to 1.5
- w_gate_up: bfloat16 [4915200], P(('dp', 'seq')), may hold values from -0.1875 to 0.1875
- w_down: bfloat16 [2457600], P(('dp', 'seq')), may hold values from -0.125 to 0.125
Outputs:
- output: bfloat16 [16, 2048, 960], P('dp', 'seq')
- input_grad: float32 [16, 2048, 960], P('dp', 'seq')
- attn_gain_grad: float32 [960], replicated
- mlp_gain_grad: float32 [960], replicated
- w_qkv_grad: float32 [1536000], P(('dp', 'seq'))
- w_out_grad: float32 [921600], P(('dp', 'seq'))
- w_gate_up_grad: float32 [4915200], P(('dp', 'seq'))
- w_down_grad: float32 [2457600], P(('dp', 'seq'))
Inputs may be any that keep to these rules, and one draw needn't show every extreme that they name: segments[r, t] is the index within row r of the first token of token t's document, so it never falls along a row and segments[r, 0] = 0; documents hold 60 to 800 tokens, a row's last one possibly fewer, except that in each aligned group of 2 rows (one index of dp) one row drawn from the seed is a single document.
All inputs are finite; a program needn't handle non-finite values.
Results may differ from a plain program's by a relative error of at most 0.014.
Values may be sent and summed in bfloat16 or wider, within the bound.
A program may use at most 576 MiB of HBM per device.

v0:
```python
import jax
import jax.numpy as jnp
from jax import lax
from jax.sharding import PartitionSpec as P

QUERY_HEADS = 15
KEY_VALUE_HEADS = 5
HEAD_WIDTH = 64


EPS = 1e-05
ROPE_BASE = 100000.0


def rotate(heads, cosine, sine):
    half = heads.shape[-1] // 2
    first = heads[..., :half]
    second = heads[..., half:]
    return jnp.concatenate(
        [first * cosine - second * sine, second * cosine + first * sine], axis=-1
    )


def norm_back(value, factor, gain, d_normed):
    gain_part = jnp.sum(d_normed * value * factor, axis=(0, 1))
    scaled = d_normed * gain
    d_value = factor * scaled - value * factor * factor * factor * jnp.mean(
        scaled * value, axis=-1, keepdims=True
    )
    return (d_value, gain_part)


def shape_weights(flat_qkv, flat_out, flat_gu, flat_down, width):
    return (
        flat_qkv.reshape(width, -1),
        flat_out.reshape(-1, width),
        flat_gu.reshape(width, -1),
        flat_down.reshape(-1, width),
    )


def local(
    tokens,
    segments,
    cotangent,
    attn_gain,
    mlp_gain,
    query_key_value_weight,
    w_out,
    w_gate_up,
    w_down,
):
    seqs, block, width = tokens.shape
    length_total = segments.shape[1]
    start = lax.axis_index("seq") * block
    gathered = (
        lax.all_gather(query_key_value_weight, ("dp", "seq"), axis=0, tiled=True),
        lax.all_gather(w_out, ("dp", "seq"), axis=0, tiled=True),
        lax.all_gather(w_gate_up, ("dp", "seq"), axis=0, tiled=True),
        lax.all_gather(w_down, ("dp", "seq"), axis=0, tiled=True),
    )
    query_key_value_matrix, wout, wgu, wdown = shape_weights(
        gathered[0], gathered[1], gathered[2], gathered[3], width
    )
    hidden_units = wgu.shape[1] // 2
    head_size = HEAD_WIDTH
    q_heads = QUERY_HEADS
    key_value_heads = KEY_VALUE_HEADS
    groups = q_heads // key_value_heads
    scale = head_size ** (-0.5)
    gain_one = attn_gain.astype(jnp.float32)
    gain_two = mlp_gain.astype(jnp.float32)
    x = tokens.astype(jnp.float32)
    rms_one = lax.rsqrt(jnp.mean(x * x, axis=-1, keepdims=True) + EPS)
    normed1 = (x * rms_one * gain_one).astype(jnp.bfloat16)
    projected = jnp.einsum(
        "scd,de->sce", normed1, query_key_value_matrix, preferred_element_type=jnp.float32
    )
    places = start + jnp.arange(block, dtype=jnp.int32)
    seg_local = lax.dynamic_slice_in_dim(segments, start, block, 1)
    position = (places[None, :] - seg_local).astype(jnp.float32)
    inverse = ROPE_BASE ** (-2.0 * jnp.arange(head_size // 2, dtype=jnp.float32) / head_size)
    angle = position[:, :, None, None] * inverse
    cosine = jnp.cos(angle)
    sine = jnp.sin(angle)
    query0 = projected[..., : q_heads * head_size].reshape(seqs, block, q_heads, head_size)
    key_initial = projected[
        ..., q_heads * head_size : (q_heads + key_value_heads) * head_size
    ].reshape(seqs, block, key_value_heads, head_size)
    value_initial = projected[..., (q_heads + key_value_heads) * head_size :].reshape(
        seqs, block, key_value_heads, head_size
    )
    query_rows = rotate(query0, cosine, sine).astype(jnp.bfloat16)
    keys = rotate(key_initial, cosine, sine).astype(jnp.bfloat16)
    values = value_initial.astype(jnp.bfloat16)
    key_all, value_all = (
        lax.all_gather(keys, "seq", axis=1, tiled=True),
        lax.all_gather(values, "seq", axis=1, tiled=True),
    )
    grouped_heads = query_rows.reshape(seqs, block, key_value_heads, groups, head_size)
    key_index = jnp.arange(length_total, dtype=jnp.int32)
    valid = (seg_local[:, :, None] == segments[:, None, :]) & (
        key_index[None, None, :] <= places[None, :, None]
    )
    valid = valid[:, None, None]

    def scores_of():
        raw = (
            jnp.einsum(
                "sqkgd,slkd->skgql", grouped_heads, key_all, preferred_element_type=jnp.float32
            )
            * scale
        )
        return jnp.where(valid, raw, -1e30)

    scores = scores_of()
    top = jnp.max(scores, axis=-1, keepdims=True)
    expo = jnp.exp(scores - top)
    total = jnp.sum(expo, axis=-1, keepdims=True)
    probs = expo / total
    log_total = top + jnp.log(total)
    mixed = jnp.einsum(
        "skgql,slkd->sqkgd",
        probs.astype(jnp.bfloat16),
        value_all,
        preferred_element_type=jnp.float32,
    )
    attn = mixed.reshape(seqs, block, q_heads * head_size).astype(jnp.bfloat16)
    hidden = x + jnp.einsum("sce,ed->scd", attn, wout, preferred_element_type=jnp.float32)
    rms_two = lax.rsqrt(jnp.mean(hidden * hidden, axis=-1, keepdims=True) + EPS)
    normed2 = (hidden * rms_two * gain_two).astype(jnp.bfloat16)
    gate_up = jnp.einsum("scd,de->sce", normed2, wgu, preferred_element_type=jnp.float32)
    gate = gate_up[..., :hidden_units]
    upper = gate_up[..., hidden_units:]
    silu_gate = jax.nn.silu(gate)
    act = (silu_gate * upper).astype(jnp.bfloat16)
    output = (
        hidden + jnp.einsum("scf,fd->scd", act, wdown, preferred_element_type=jnp.float32)
    ).astype(jnp.bfloat16)
    again = (
        lax.all_gather(query_key_value_weight, ("dp", "seq"), axis=0, tiled=True),
        lax.all_gather(w_out, ("dp", "seq"), axis=0, tiled=True),
        lax.all_gather(w_gate_up, ("dp", "seq"), axis=0, tiled=True),
        lax.all_gather(w_down, ("dp", "seq"), axis=0, tiled=True),
    )
    query_key_value_matrix, wout, wgu, wdown = shape_weights(
        again[0], again[1], again[2], again[3], width
    )
    grad_down = jnp.einsum("scf,scd->fd", act, cotangent, preferred_element_type=jnp.float32)
    d_act = jnp.einsum("scd,fd->scf", cotangent, wdown, preferred_element_type=jnp.float32)
    sigma = jax.nn.sigmoid(gate)
    d_gate = d_act * upper * sigma * (1.0 + gate * (1.0 - sigma))
    d_upper = d_act * silu_gate
    d_gate_up = jnp.concatenate([d_gate, d_upper], axis=-1).astype(jnp.bfloat16)
    grad_gate_up = jnp.einsum("scd,sce->de", normed2, d_gate_up, preferred_element_type=jnp.float32)
    d_normed2 = jnp.einsum("sce,de->scd", d_gate_up, wgu, preferred_element_type=jnp.float32)
    d_from_norm, grad_gain_two = norm_back(hidden, rms_two, gain_two, d_normed2)
    d_hidden = cotangent.astype(jnp.float32) + d_from_norm
    d_hid_low = d_hidden.astype(jnp.bfloat16)
    grad_out = jnp.einsum("sce,scd->ed", attn, d_hid_low, preferred_element_type=jnp.float32)
    d_attn = jnp.einsum("scd,ed->sce", d_hid_low, wout, preferred_element_type=jnp.float32).astype(
        jnp.bfloat16
    )
    d_grouped = d_attn.reshape(seqs, block, key_value_heads, groups, head_size)
    probs = jnp.exp(scores_of() - log_total)
    d_probs = jnp.einsum(
        "sqkgd,slkd->skgql", d_grouped, value_all, preferred_element_type=jnp.float32
    )
    inner = jnp.sum(probs * d_probs, axis=-1, keepdims=True)
    d_scores = (probs * (d_probs - inner)).astype(jnp.bfloat16)
    d_query = (
        jnp.einsum("skgql,slkd->sqkgd", d_scores, key_all, preferred_element_type=jnp.float32)
        * scale
    )
    d_key_all = (
        jnp.einsum("skgql,sqkgd->slkd", d_scores, grouped_heads, preferred_element_type=jnp.float32)
        * scale
    )
    d_value_all = jnp.einsum(
        "skgql,sqkgd->slkd",
        probs.astype(jnp.bfloat16),
        d_grouped,
        preferred_element_type=jnp.float32,
    )
    d_key, d_value = (
        lax.psum_scatter(
            d_key_all.astype(jnp.bfloat16), "seq", scatter_dimension=1, tiled=True
        ).astype(jnp.float32),
        lax.psum_scatter(
            d_value_all.astype(jnp.bfloat16), "seq", scatter_dimension=1, tiled=True
        ).astype(jnp.float32),
    )
    d_query = rotate(d_query.reshape(seqs, block, q_heads, head_size), cosine, -sine)
    d_key = rotate(d_key, cosine, -sine)
    d_proj = jnp.concatenate(
        [
            d_query.reshape(seqs, block, -1),
            d_key.reshape(seqs, block, -1),
            d_value.reshape(seqs, block, -1),
        ],
        axis=-1,
    ).astype(jnp.bfloat16)
    grad_qkv = jnp.einsum("scd,sce->de", normed1, d_proj, preferred_element_type=jnp.float32)
    d_normed1 = jnp.einsum(
        "sce,de->scd", d_proj, query_key_value_matrix, preferred_element_type=jnp.float32
    )
    d_from_first, grad_gain_one = norm_back(x, rms_one, gain_one, d_normed1)
    input_grad = d_hidden + d_from_first
    gain_one_total, gain_two_total = lax.psum((grad_gain_one, grad_gain_two), ("dp", "seq"))
    flat = (
        grad_qkv.reshape(-1),
        grad_out.reshape(-1),
        grad_gate_up.reshape(-1),
        grad_down.reshape(-1),
    )
    owned = (
        lax.psum_scatter(flat[0], ("dp", "seq"), scatter_dimension=0, tiled=True),
        lax.psum_scatter(flat[1], ("dp", "seq"), scatter_dimension=0, tiled=True),
        lax.psum_scatter(flat[2], ("dp", "seq"), scatter_dimension=0, tiled=True),
        lax.psum_scatter(flat[3], ("dp", "seq"), scatter_dimension=0, tiled=True),
    )
    return (
        output,
        input_grad,
        gain_one_total,
        gain_two_total,
        owned[0],
        owned[1],
        owned[2],
        owned[3],
    )


def solution(mesh):
    placed = (
        P("dp", "seq", None),
        P("dp", None),
        P("dp", "seq", None),
        P(),
        P(),
        P(("dp", "seq")),
        P(("dp", "seq")),
        P(("dp", "seq")),
        P(("dp", "seq")),
    )
    return jax.shard_map(
        local,
        mesh=mesh,
        in_specs=placed,
        out_specs=(
            P("dp", "seq", None),
            P("dp", "seq", None),
            P(),
            P(),
            P(("dp", "seq")),
            P(("dp", "seq")),
            P(("dp", "seq")),
            P(("dp", "seq")),
        ),
        check_vma=False,
    )
```

profile of v0, /device:TPU:0, one launch (start us, length us, event | category | flops | bytes accessed | tf_op | source)
XLA Modules:
  0.0 1449.1 jit_solution(17075148050082230648)
XLA Ops:
  15.9 67.5 %all-gather.17.cloned.1.call-done = bf16[32,1,48000]{2,1,0:T(2,128)(2,1)} async-done(((bf16[1,1,48000]{2,1,0:T(2,128)(2,1)}), bf16[32,1,48000]{2,1,0:T(2,128)(2,1)}) %all-gather.17.cloned.1.call-update) | async-done | bytes 3072016 | tf_op jit(solution)/shard_map/all_gather | solution.py:57
  83.4 18.4 %reduce = bf16[32,48000]{1,0:T(8,128)(2,1)S(1)} reduce(bf16[32,1,48000]{2,1,0:T(2,128)(2,1)} %all-gather.17.cloned.1.call-done, bf16[]{:T(256)} %constant.54), dimensions={1}, to_apply=%all-gather.reduce_sub_computation | reduce | bytes 6144002 | tf_op jit(solution)/shard_map/all_gather | solution.py:57
  106.2 6.4 fusion.55
  124.1 21.8 %all-gather.19.cloned.1.call-done = bf16[32,1,28800]{2,1,0:T(2,128)(2,1)} async-done(((bf16[1,1,28800]{2,1,0:T(2,128)(2,1)}), bf16[32,1,28800]{2,1,0:T(2,128)(2,1)}) %all-gather.19.cloned.1.call-update) | async-done | bytes 1843216 | tf_op jit(solution)/shard_map/all_gather | solution.py:58
  145.9 39.5 %reduce.1 = bf16[32,28800]{1,0:T(8,128)(2,1)S(1)} reduce(bf16[32,1,28800]{2,1,0:T(2,128)(2,1)} %all-gather.19.cloned.1.call-done, bf16[]{:T(256)} %constant.54), dimensions={1}, to_apply=%all-gather.1.reduce_sub_computation | reduce | bytes 3686402 | tf_op jit(solution)/shard_map/all_gather | solution.py:58
  194.5 17.4 %all-gather.15.cloned.1.call-done = bf16[2457600]{0:T(1024)(128)(2,1)} async-done(((bf16[76800]{0:T(1024)(128)(2,1)}), bf16[2457600]{0:T(1024)(128)(2,1)}) %all-gather.15.cloned.1.call-update) | async-done | bytes 4915216 | tf_op jit(solution)/shard_map/all_gather | solution.py:60
  212.0 9.6 reshape.173
  221.6 46.0 %all-gather.11.cloned.1.call-done = bf16[2,2048,5,64]{1,3,2,0:T(8,128)(2,1)} async-done(((bf16[2,512,5,64]{1,3,2,0:T(8,128)(2,1)}), bf16[2,2048,5,64]{1,3,2,0:T(8,128)(2,1)}) %all-gather.11.cloned.1.call-update) | async-done | bytes 2621456 | tf_op jit(solution)/shard_map/all_gather | solution.py:97
  267.6 46.2 %fusion.65 = (f32[2,5,3,512]{3,2,1,0:T(4,128)S(1)}, f32[2,5,3,512,2048]{3,4,2,1,0:T(8,128)}) fusion(bf16[2,512,5,3,32]{1,4,3,2,0:T(8,128)(2,1)S(1)} %bitcast.115, bf16[2,512,5,3,32]{1,4,3,2,0:T(8,128)(2,1)S(1)} %bitcast.113, bf16[2,2048,5,64]{1,3,2,0:T(8,128)(2,1)} %all-gather.11.cloned.1.call-done, pred[2,512,2048]{1,2,0:T(8,128)(4,1)} %compare_and_fusion), kind=kOutput, calls=%fused_computation.106 | convolution fusion | flops 4124820480 | bytes 132575232 | tf_op jit(solution)/shard_map/sqkgd,slkd->skgql/dot_general | solution.py:109
  313.8 38.4 %fusion.3 = f32[2,5,3,512]{3,2,1,0:T(4,128)S(1)} fusion(f32[2,5,3,512,2048]{3,4,2,1,0:T(8,128)} %get-tuple-element.35, f32[2,5,3,512]{3,2,1,0:T(4,128)S(1)} %get-tuple-element.34), kind=kLoop, calls=%fused_computation.9 | loop fusion | flops 62899200 | bytes 125952000 | tf_op jit(solution)/shard_map/reduce_sum | solution.py:119
  352.2 44.7 %fusion.48 = bf16[2,5,64,3,512]{4,2,3,1,0:T(8,128)(2,1)} fusion(f32[2,5,3,512,2048]{3,4,2,1,0:T(8,128)} %get-tuple-element.35, f32[2,5,3,512]{3,2,1,0:T(4,128)S(1)} %fusion.3, f32[2,5,3,512]{3,2,1,0:T(4,128)S(1)} %get-tuple-element.34, bf16[2,2048,5,64]{1,3,2,0:T(8,128)(2,1)} %all-gather.9.cloned.1.call-done), kind=kOutput, calls=%fused_computation.75 | convolution fusion | flops 4121886720 | bytes 130539520 | tf_op jit(solution)/shard_map/skgql,slkd->sqkgd/dot_general | solution.py:122
  396.9 6.5 multiply_reduce_fusion.2
  407.9 14.9 %reshape.193 = bf16[960,5120,1]{1,0,2:T(8,128)(2,1)} reshape(bf16[4915200]{0:T(1024)(128)(2,1)} %all-gather.13.cloned.1.call-done) | data formatting | bytes 19660800 | tf_op jit(solution)/shard_map/reshape | solution.py:37
  422.8 19.4 %fusion.64 = f32[2,512,5120]{2,1,0:T(8,128)} fusion(bf16[960,5120,1]{1,0,2:T(8,128)(2,1)} %reshape.193, f32[2,512,960]{1,2,0:T(8,128)} %get-tuple-element.37, f32[960]{0:T(1024)S(1)} %copy-done.19, f32[2,512]{1,0:T(2,128)S(1)} %add_rsqrt_fusion), kind=kOutput, calls=%fused_computation.105 | convolution fusion | flops 10069278720 | bytes 34742016 | tf_op jit(solution)/shard_map/scd,de->sce/dot_general | solution.py:132
  442.2 18.6 %multiply_convert_fusion.1 = (bf16[2,512,2560]{2,1,0:T(8,128)(2,1)}, bf16[2,512,2560]{2,1,0:T(8,128)(2,1)}, bf16[2,512,2560]{2,1,0:T(8,128)(2,1)}) fusion(f32[2,512,5120]{2,1,0:T(8,128)} %fusion.64, bf16[2,512,960]{1,2,0:T(8,128)(2,1)S(1)} %copy-done.10, bf16[2560,960]{1,0:T(8,128)(2,1)} %reshape.173), kind=kOutput, calls=%fused_computation.16 | convolution fusion | flops 5072486400 | bytes 43581440 | tf_op jit(solution)/shard_map/scd,fd->scf/dot_general | solution.py:150
  460.8 19.0 %multiply_reduce_fusion = (f32[960]{0:T(1024)}, f32[2,512]{1,0:T(2,128)S(1)}, f32[2,512,960]{1,2,0:T(8,128)}) fusion(f32[2,512,960]{1,2,0:T(8,128)} %get-tuple-element.37, f32[2,512]{1,0:T(2,128)S(1)} %add_rsqrt_fusion, f32[960]{0:T(1024)S(1)} %copy-done.19, bf16[960,5120,1]{1,0,2:T(8,128)(2,1)} %reshape.193, bf16[2,512,2560]{2,1,0:T(8,128)(2,1)} %get-tuple-element.21, ...), kind=kOutput, calls=%fused_computation.49 | convolution fusion | flops 10093197312 | bytes 28196352 | tf_op jit(solution)/shard_map/sce,de->scd/dot_general | solution.py:156
  479.8 19.0 %convolution_bitcast_fusion = f32[120,40,8,128]{3,2,1,0:T(8,128)} fusion(bf16[2,512,2560]{2,1,0:T(8,128)(2,1)} %get-tuple-element.21, bf16[2,512,2560]{2,1,0:T(8,128)(2,1)} %get-tuple-element.20, f32[2,512,960]{1,2,0:T(8,128)} %get-tuple-element.37, f32[960]{0:T(1024)S(1)} %copy-done.19, f32[2,512]{1,0:T(2,128)S(1)} %add_rsqrt_fusion), kind=kOutput, calls=%fused_computation.20 | convolution fusion | flops 10090250240 | bytes 34086656 | tf_op jit(solution)/shard_map/scd,sce->de/dot_general | solution.py:155
  505.7 86.1 %fusion = (f32[2,5,3,512]{3,2,1,0:T(4,128)S(1)}, f32[2,5,2048,512,3]{3,2,4,1,0:T(8,128)}) fusion(f32[2,5,3,512,2048]{3,4,2,1,0:T(8,128)} %get-tuple-element.35, f32[2,5,3,512]{3,2,1,0:T(4,128)S(1)} %log_add_fusion, bf16[2,512,5,3,64]{1,4,3,2,0:T(8,128)(2,1)S(1)} %bitcast.110, bf16[2,2048,5,64]{1,3,2,0:T(8,128)(2,1)} %all-gather.9.cloned.1.call-done), kind=kOutput, calls=%fused_computation.2 | convolution fusion | flops 4120888320 | bytes 256368640 | tf_op jit(solution)/shard_map/sqkgd,slkd->skgql/dot_general | solution.py:166
  591.8 96.6 %fusion.2 = bf16[2,5,3,512,2048]{3,4,2,1,0:T(8,128)(2,1)} fusion(f32[2,5,2048,512,3]{3,2,4,1,0:T(8,128)} %get-tuple-element.40, f32[2,5,3,512,2048]{3,4,2,1,0:T(8,128)} %get-tuple-element.35, f32[2,5,3,512]{3,2,1,0:T(4,128)S(1)} %get-tuple-element.39, f32[2,5,3,512]{3,2,1,0:T(4,128)S(1)} %log_add_fusion), kind=kLoop, calls=%fused_computation.4 | loop fusion | flops 125829120 | bytes 314695680 | tf_op jit(solution)/shard_map/convert_element_type | solution.py:170
  688.4 27.5 %fusion.29 = bf16[2,2048,5,64]{1,3,2,0:T(8,128)(2,1)} fusion(bf16[2,5,3,512,2048]{3,4,2,1,0:T(8,128)(2,1)} %fusion.2, bf16[2,512,5,3,32]{1,4,3,2,0:T(8,128)(2,1)} %bitcast.116, bf16[2,512,5,3,32]{1,4,3,2,0:T(8,128)(2,1)S(1)} %bitcast.114), kind=kOutput, calls=%fused_computation.56 | convolution fusion | flops 4033085440 | bytes 67502080 | tf_op jit(solution)/shard_map/skgql,sqkgd->slkd/dot_general | solution.py:176
  716.0 10.5 convolution_bitcast_fusion.1
  726.5 42.0 %fusion.30 = bf16[2,2048,5,64]{1,3,2,0:T(8,128)(2,1)} fusion(bf16[2,512,5,3,64]{1,4,3,2,0:T(8,128)(2,1)S(1)} %bitcast.111, f32[2,5,3,512,2048]{3,4,2,1,0:T(8,128)} %get-tuple-element.35, f32[2,5,3,512]{3,2,1,0:T(4,128)S(1)} %log_add_fusion), kind=kOutput, calls=%fused_computation.57 | convolution fusion | flops 4090757120 | bytes 130478080 | tf_op jit(solution)/shard_map/skgql,sqkgd->slkd/dot_general | solution.py:179
  768.8 6.9 convolution_bitcast_fusion.3
  781.1 18.5 %copy.62 = f32[120,40,8,128]{3,1,2,0:T(8,128)} copy(f32[120,40,8,128]{3,2,1,0:T(8,128)} %convolution_bitcast_fusion) | data formatting | bytes 39321600
  799.7 13.1 reshape.182
  812.8 25.8 %fusion.39 = f32[2,5,64,3,512]{4,2,3,1,0:T(8,128)} fusion(bf16[2,5,3,512,2048]{3,4,2,1,0:T(8,128)(2,1)} %fusion.2, bf16[2,2048,5,64]{1,3,2,0:T(8,128)(2,1)} %all-gather.11.cloned.1.call-done), kind=kOutput, calls=%fused_computation.64 | convolution fusion | flops 4027514880 | bytes 69468160 | tf_op jit(solution)/shard_map/skgql,slkd->sqkgd/dot_general | solution.py:172
  844.6 8.3 convolution_bitcast_fusion.2
  852.9 8.2 reshape.179
  861.2 10.7 add_convert_fusion
  877.5 41.0 %all-reduce.4 = (f32[960]{0:T(1024)}, f32[960]{0:T(1024)}) all-reduce(f32[960]{0:T(1024)S(1)} %get-tuple-element.10, f32[960]{0:T(1024)S(1)} %copy-done.20), channel_id=1, replica_groups=mesh['dp'=8,'seq'=4] {'dp','seq'}, use_global_device_ids=true, to_apply=%region_10.11 | all-reduce | flops 1920 | bytes 15360 | tf_op jit(solution)/shard_map/psum | solution.py:209
  918.6 6.6 fusion.22
  925.2 510.1 %all-reduce.8.cloned.1.call-done = (f32[1536000]{0:T(1024)}, f32[921600]{0:T(1024)}, f32[4915200]{0:T(1024)}, f32[2457600]{0:T(1024)}) async-done(((f32[1536000]{0:T(1024)}, f32[921600]{0:T(1024)}, f32[4915200]{0:T(1024)}, f32[2457600]{0:T(1024)}), (f32[1536000]{0:T(1024)}, f32[921600]{0:T(1024)}, f32[4915200]{0:T(1024)}, f32[2457600]{0:T(1024)})) %all-reduce.8.cloned.1.call-update) | async-done | bytes 39321616
  (107 shorter events, 69.2 us)
Async XLA Ops:
  7.2 76.2 %all-gather.17.cloned.1.call-start = ((), (), s32[]{:S(2)}) async-start(), calls=%async_computation.8 | async-start | bytes 6336000 | tf_op jit(solution)/shard_map/all_gather | solution.py:57
  8.9 137.0 %all-gather.19.cloned.1.call-start = ((), (), s32[]{:S(2)}) async-start(), calls=%async_computation.9 | async-start | bytes 3801600 | tf_op jit(solution)/shard_map/all_gather | solution.py:58
  10.5 201.5 %all-gather.15.cloned.1.call-start = ((), (), s32[]{:S(2)}) async-start(), calls=%async_computation.5 | async-start | bytes 5068800 | tf_op jit(solution)/shard_map/all_gather | solution.py:60
  11.3 256.3 %all-gather.11.cloned.1.call-start = ((), (), s32[]{:S(2)}) async-start(), calls=%async_computation.3 | async-start | bytes 3276800 | tf_op jit(solution)/shard_map/all_gather | solution.py:97
  12.0 94.2 %copy-start.15 = (f32[960]{0:T(1024)}, f32[960]{0:T(1024)S(1)}, u32[]{:S(2)}) copy-start(f32[960]{0:T(1024)S(1)} %convert_element_type.79) | copy-start | bytes 11524
  14.0 92.2 %copy-start.17 = (f32[2,512]{1,0:T(2,128)}, f32[2,512]{1,0:T(2,128)S(1)}, u32[]{:S(2)}) copy-start(f32[2,512]{1,0:T(2,128)S(1)} %add_rsqrt_fusion.1) | copy-start | bytes 12292
  15.9 175.1 %copy-start.7 = (f32[2,512,32]{1,2,0:T(8,128)}, f32[2,512,32]{1,2,0:T(8,128)S(1)}, u32[]{:S(2)}) copy-start(f32[2,512,32]{1,2,0:T(8,128)S(1)} %get-tuple-element.33) | copy-start | bytes 393220
  112.6 2.7 copy-start.1
  115.4 5.0 copy-start.21
  115.4 5.6 copy-start.14
  116.5 235.7 %all-gather.9.cloned.1.call-start = ((), (), s32[]{:S(2)}) async-start(), calls=%async_computation.2 | async-start | bytes 3276800 | tf_op jit(solution)/shard_map/all_gather | solution.py:98
  118.9 289.0 %all-gather.13.cloned.1.call-start = ((), (), s32[]{:S(2)}) async-start(), calls=%async_computation.4 | async-start | bytes 10137600 | tf_op jit(solution)/shard_map/all_gather | solution.py:59
  119.5 723.6 %reduce-scatter.3.cloned.1.call-start = ((), (), s32[]{:S(2)}) async-start(), calls=%async_computation.6 | async-start | bytes 3276800 | tf_op jit(solution)/shard_map/reduce_scatter | solution.py:186
  191.0 2.8 slice-start
  194.5 73.1 %copy-start.4 = (bf16[2,512,15,32]{1,3,2,0:T(8,128)(2,1)}, bf16[2,512,15,32]{1,3,2,0:T(8,128)(2,1)S(1)}, u32[]{:S(2)}) copy-start(bf16[2,512,15,32]{1,3,2,0:T(8,128)(2,1)S(1)} %get-tuple-element.25) | copy-start | bytes 2949124
  194.5 73.1 %copy-start.6 = (bf16[2,512,15,32]{1,3,2,0:T(8,128)(2,1)}, bf16[2,512,15,32]{1,3,2,0:T(8,128)(2,1)S(1)}, u32[]{:S(2)}) copy-start(bf16[2,512,15,32]{1,3,2,0:T(8,128)(2,1)S(1)} %get-tuple-element.26) | copy-start | bytes 2949124
  352.2 44.7 %copy-start.2 = (bf16[2,512,960]{1,2,0:T(8,128)(2,1)S(1)}, bf16[2,512,960]{1,2,0:T(8,128)(2,1)}, u32[]{:S(2)}) copy-start(bf16[2,512,960]{1,2,0:T(8,128)(2,1)} %param.9) | copy-start | bytes 5898244
  403.4 19.4 %copy-start.19 = (f32[960]{0:T(1024)S(1)}, f32[960]{0:T(1024)}, u32[]{:S(2)}) copy-start(f32[960]{0:T(1024)} %convert_element_type.87) | copy-start | bytes 11524
  422.8 19.4 %copy-start.10 = (bf16[2,512,960]{1,2,0:T(8,128)(2,1)S(1)}, bf16[2,512,960]{1,2,0:T(8,128)(2,1)}, u32[]{:S(2)}) copy-start(bf16[2,512,960]{1,2,0:T(8,128)(2,1)} %param.11) | copy-start | bytes 5898244
  498.8 4.6 copy-start.12
  591.8 96.6 %copy-start.5 = (bf16[2,512,15,32]{1,3,2,0:T(8,128)(2,1)S(1)}, bf16[2,512,15,32]{1,3,2,0:T(8,128)(2,1)}, u32[]{:S(2)}) copy-start(bf16[2,512,15,32]{1,3,2,0:T(8,128)(2,1)} %copy-done.4) | copy-start | bytes 2949124
  715.9 128.6 %reduce-scatter.5.cloned.1.call-start = ((), (), s32[]{:S(2)}) async-start(), calls=%async_computation.7 | async-start | bytes 3276800 | tf_op jit(solution)/shard_map/reduce_scatter | solution.py:189
  768.6 666.8 %all-reduce.8.cloned.1.call-start = ((), (), s32[]{:S(2)}) async-start(), calls=%async_computation.10 | async-start | bytes 78643200
  812.8 25.8 %copy-start.8 = (f32[2,512,32]{1,2,0:T(8,128)S(1)}, f32[2,512,32]{1,2,0:T(8,128)}, u32[]{:S(2)}) copy-start(f32[2,512,32]{1,2,0:T(8,128)} %copy-done.7) | copy-start | bytes 393220
  812.8 25.8 %copy-start.13 = (f32[2,512,32]{1,2,0:T(8,128)S(1)}, f32[2,512,32]{1,2,0:T(8,128)}, u32[]{:S(2)}) copy-start(f32[2,512,32]{1,2,0:T(8,128)} %get-tuple-element.31) | copy-start | bytes 393220
  841.4 3.2 copy-start.3
  841.4 3.2 copy-start.16
  841.4 3.2 copy-start.18
  861.1 10.7 copy-start.9
  861.2 10.7 copy-start.11
  861.2 10.7 copy-start.22
  871.9 5.6 copy-start.20
  (1 other events, 2.2 us)
Sparse Core Ops, SparseCore 0:
  11.5 71.8 all-gather.16
  86.8 59.0 all-gather.18
  148.8 63.1 all-gather.14
  214.0 53.5 all-gather.10
  269.0 53.5 all-gather.8
  325.3 82.5 all-gather.12
  716.1 50.7 reduce-scatter.2
  769.2 51.7 reduce-scatter.4
  861.3 574.0 all-reduce.7
where the time goes:
time: 1460 us; the launch traced here: 1450 us
  waiting for transfers between devices  669 us (46%)
  matrix products  405 us (28%)
  other arithmetic  221 us (15%)
  local copies, waits for them, and re-layouts  97.9 us (7%)
  blocking collectives  41 us (3%)
    unnamed x10, waiting for transfers between devices  511 us
    convert_element_type x1, other arithmetic, local(): d_scores = (probs * (d_probs - inner)).astype(jnp.bfloat16)  96.6 us
    dot_general x1, matrix products, local(): jnp.einsum('sqkgd,slkd->skgql', d_grouped, value_all, preferred_element_t...  86.1 us
    all_gather x1, waiting for transfers between devices, local(): lax.all_gather(query_key_value_weight, ('dp', 'seq'), axis=0, tiled=True)  67.5 us
    dot_general x1, matrix products, scores_of(): jnp.einsum('sqkgd,slkd->skgql', grouped_heads, key_all, preferred_element...  46.2 us
    all_gather x1, waiting for transfers between devices, local(): lax.all_gather(keys, 'seq', axis=1, tiled=True)  46 us
    dot_general x1, matrix products, local(): jnp.einsum('skgql,slkd->sqkgd', probs.astype(jnp.bfloat16), value_all, pr...  44.7 us
    dot_general x1, matrix products, local(): jnp.einsum('skgql,sqkgd->slkd', probs.astype(jnp.bfloat16), d_grouped, pr...  42 us
  transfers between devices with their start and end apart: 9, of which 6 were waited for; matrix products, arithmetic and copies ran while one was open for 27% of the time, Pallas kernels for 0%

commit v1 on v0

v1 whole, which is shorter than its diff:
```python
import functools

import jax
import jax.numpy as jnp
from jax import lax
from jax.experimental import pallas as pl
from jax.experimental.pallas import tpu as pltpu
from jax.sharding import PartitionSpec as P

QUERY_HEADS = 15
KEY_VALUE_HEADS = 5
HEAD_WIDTH = 64
GROUPS = QUERY_HEADS // KEY_VALUE_HEADS

EPS = 1e-05
ROPE_BASE = 100000.0
SCALE = HEAD_WIDTH ** (-0.5)
SCALE_LOG2 = SCALE * 1.4426950408889634
KEY_TILE = 512
QUERY_TILE = 512
FORWARD_QUERY_TILE = 512

F32 = jnp.float32
BF16 = jnp.bfloat16


def rotate(heads, cosine, sine):
    half = heads.shape[2] // 2
    first = heads[:, :, :half]
    second = heads[:, :, half:]
    return jnp.concatenate(
        [first * cosine - second * sine, second * cosine + first * sine], axis=2
    )


def norm_back(value, factor, gain, d_normed):
    gain_part = jnp.sum(d_normed * value * factor, axis=(0, 1))
    scaled = d_normed * gain
    d_value = factor * scaled - value * factor * factor * factor * jnp.mean(
        scaled * value, axis=-1, keepdims=True
    )
    return (d_value, gain_part)


def gather_weight(flat, width):
    if flat.shape[0] % width == 0:
        return lax.all_gather(flat.reshape(-1, width), ("dp", "seq"), axis=0, tiled=True)
    return lax.all_gather(flat, ("dp", "seq"), axis=0, tiled=True).reshape(-1, width)


def dot(left, right, dims):
    return lax.dot_general(left, right, (dims, ((), ())), preferred_element_type=F32)


def valid_keys(index, seg, q_index, me, block, tile, q_tile):
    keys = index * tile + lax.broadcasted_iota(jnp.int32, (tile, q_tile), 0)
    first = me * block + q_index * q_tile
    query = first + lax.broadcasted_iota(jnp.int32, (1, q_tile), 1)
    return (keys >= seg) & (keys <= query)


def key_range(low_ref, q_index, me, block, tile, q_tile):
    return low_ref[q_index], (me * block + (q_index + 1) * q_tile + tile - 1) // tile


def attend_kernel(block, tile, q_tile, me_ref, low_ref, q_ref, kv_ref, seg_ref, out_ref, lse_ref):
    q_index = pl.program_id(1)
    me = me_ref[0]
    parts = block // tile
    seg = seg_ref[...]

    def step(index, state):
        slot = me - index // parts
        part = lax.rem(index, parts)
        where = pl.ds(pl.multiple_of(part * tile, tile), tile)
        keys = kv_ref[slot, 0, 0, :, where]
        values = kv_ref[slot, 1, 0, :, where]
        valid = valid_keys(index, seg, q_index, me, block, tile, q_tile)
        out = []
        for head in range(GROUPS):
            top, total, mixed = state[head]
            scores = dot(keys, q_ref[head], ((0,), (0,))) * SCALE_LOG2
            scores = jnp.where(valid, scores, -1e30)
            new_top = jnp.maximum(top, jnp.max(scores, axis=0, keepdims=True))
            probs = jnp.exp2(scores - new_top)
            shrink = jnp.exp2(top - new_top)
            total = total * shrink + jnp.sum(probs, axis=0, keepdims=True)
            mixed = mixed * shrink + dot(values, probs.astype(BF16), ((1,), (0,)))
            out.append((new_top, total, mixed))
        return tuple(out)

    first = (
        jnp.full((1, q_tile), -1e30, F32),
        jnp.zeros((1, q_tile), F32),
        jnp.zeros((HEAD_WIDTH, q_tile), F32),
    )
    begin, end = key_range(low_ref, q_index, me, block, tile, q_tile)
    state = lax.fori_loop(begin, end, step, (first,) * GROUPS)
    for head in range(GROUPS):
        top, total, mixed = state[head]
        out_ref[head] = (mixed / total).astype(BF16)
        lse_ref[head] = top + jnp.log2(total)


def attend_back_kernel(
    block, tile, q_tile, steps, me_ref, low_ref, q_ref, kv_ref, seg_ref, out_ref, lse_ref, d_out_ref,
    d_q_ref, d_kv_ref, sums
):
    q_index = pl.program_id(1)
    me = me_ref[0]
    parts = block // tile
    seg = seg_ref[...]

    @pl.when(q_index == 0)
    def _():
        sums[...] = jnp.zeros_like(sums)

    inner = [
        jnp.sum(d_out_ref[head].astype(F32) * out_ref[head].astype(F32), axis=0, keepdims=True)
        for head in range(GROUPS)
    ]

    def step(index, state):
        slot = me - index // parts
        part = lax.rem(index, parts)
        where = pl.ds(pl.multiple_of(part * tile, tile), tile)
        keys = kv_ref[slot, 0, 0, :, where]
        values = kv_ref[slot, 1, 0, :, where]
        valid = valid_keys(index, seg, q_index, me, block, tile, q_tile)
        out = []
        d_key = jnp.zeros((HEAD_WIDTH, tile), F32)
        d_value = jnp.zeros((HEAD_WIDTH, tile), F32)
        for head in range(GROUPS):
            query = q_ref[head]
            d_out = d_out_ref[head]
            scores = dot(keys, query, ((0,), (0,))) * SCALE_LOG2
            probs = jnp.exp2(jnp.where(valid, scores, -1e30) - lse_ref[head])
            d_probs = dot(values, d_out, ((0,), (0,)))
            d_scores = (probs * (d_probs - inner[head])).astype(BF16)
            out.append(state[head] + dot(keys, d_scores, ((1,), (0,))))
            d_key += dot(query, d_scores, ((1,), (1,)))
            d_value += dot(d_out, probs.astype(BF16), ((1,), (1,)))
        sums[slot, 0, :, where] += d_key
        sums[slot, 1, :, where] += d_value
        return tuple(out)

    begin, end = key_range(low_ref, q_index, me, block, tile, q_tile)
    state = lax.fori_loop(
        begin, end, step, (jnp.zeros((HEAD_WIDTH, q_tile), F32),) * GROUPS
    )
    for head in range(GROUPS):
        d_q_ref[head] = (state[head] * SCALE).astype(d_q_ref.dtype)

    @pl.when(q_index == steps - 1)
    def _():
        d_kv_ref[:, 0, 0] = (sums[:, 0] * SCALE).astype(d_kv_ref.dtype)
        d_kv_ref[:, 1, 0] = sums[:, 1].astype(d_kv_ref.dtype)


def low_tiles(seg, tile, q_tile):
    return seg[0, ::q_tile] // tile


def attention_specs(slots, block, tile):
    heads = pl.BlockSpec((GROUPS, HEAD_WIDTH, tile), lambda g, q, *_: (g, 0, q))
    kv = pl.BlockSpec((slots, 2, 1, HEAD_WIDTH, block), lambda g, q, *_: (0, 0, g, 0, 0))
    seg = pl.BlockSpec((1, tile), lambda g, q, *_: (0, q))
    lse = pl.BlockSpec((GROUPS, 1, tile), lambda g, q, *_: (g, 0, q))
    return heads, kv, seg, lse


def attend(me, query, kv, seg):
    slots, block = kv.shape[0], query.shape[-1]
    tile, q_tile = min(KEY_TILE, block), min(FORWARD_QUERY_TILE, block)
    low = low_tiles(seg, tile, q_tile)
    heads, kv_spec, seg_spec, lse = attention_specs(slots, block, q_tile)
    work = QUERY_HEADS * block * slots * block
    return pl.pallas_call(
        functools.partial(attend_kernel, block, tile, q_tile),
        grid_spec=pltpu.PrefetchScalarGridSpec(
            num_scalar_prefetch=2,
            grid=(KEY_VALUE_HEADS, block // q_tile),
            in_specs=[heads, kv_spec, seg_spec],
            out_specs=[heads, lse],
        ),
        out_shape=[
            jax.ShapeDtypeStruct(query.shape, BF16),
            jax.ShapeDtypeStruct((QUERY_HEADS, 1, block), F32),
        ],
        compiler_params=pltpu.CompilerParams(vmem_limit_bytes=40 * 2**20),
        cost_estimate=pl.CostEstimate(
            flops=16 * work * HEAD_WIDTH, bytes_accessed=8 * 2**20, transcendentals=work
        ),
        name="attend",
    )(me, low, query, kv, seg)


def attend_back(me, query, kv, seg, attn, lse_rows, d_attn):
    slots, block = kv.shape[0], query.shape[-1]
    tile, q_tile = min(KEY_TILE, block), min(QUERY_TILE, block)
    low = low_tiles(seg, tile, q_tile)
    heads, kv_spec, seg_spec, lse = attention_specs(slots, block, q_tile)
    work = QUERY_HEADS * block * slots * block
    return pl.pallas_call(
        functools.partial(attend_back_kernel, block, tile, q_tile, block // q_tile),
        grid_spec=pltpu.PrefetchScalarGridSpec(
            num_scalar_prefetch=2,
            grid=(KEY_VALUE_HEADS, block // q_tile),
            in_specs=[heads, kv_spec, seg_spec, heads, lse, heads],
            out_specs=[heads, kv_spec],
            scratch_shapes=[pltpu.VMEM((slots, 2, HEAD_WIDTH, block), F32)],
        ),
        out_shape=[
            jax.ShapeDtypeStruct(query.shape, F32),
            jax.ShapeDtypeStruct(kv.shape, BF16),
        ],
        compiler_params=pltpu.CompilerParams(vmem_limit_bytes=40 * 2**20),
        cost_estimate=pl.CostEstimate(
            flops=40 * work * HEAD_WIDTH, bytes_accessed=16 * 2**20, transcendentals=work
        ),
        name="attend_back",
    )(me, low, query, kv, seg, attn, lse_rows, d_attn)


def from_before(own, slots):
    held = [own]
    for slot in range(1, slots):
        pairs = [(i, i + slot) for i in range(slots - slot)]
        held.append(lax.ppermute(own, "seq", pairs))
    return jnp.stack(held)


def sum_to_owner(parts, slots):
    total = parts[0].astype(F32)
    for slot in range(1, slots):
        pairs = [(i + slot, i) for i in range(slots - slot)]
        total += lax.ppermute(parts[slot], "seq", pairs).astype(F32)
    return total


def scatter_sum(grad, dp, seq):
    rows, width = grad.shape
    part = lax.psum_scatter(grad, "dp", scatter_dimension=0, tiled=True)
    if (rows // dp) % seq != 0:
        part = part.reshape(seq, -1)
    else:
        part = part.reshape(seq, rows // dp // seq, width)
    owned = lax.psum_scatter(part, "seq", scatter_dimension=0, tiled=False)
    return owned.astype(F32).reshape(-1)


def local(
    dp,
    slots,
    tokens,
    segments,
    cotangent,
    attn_gain,
    mlp_gain,
    query_key_value_weight,
    w_out,
    w_gate_up,
    w_down,
):
    seqs, block, width = tokens.shape
    me = lax.axis_index("seq")
    start = me * block
    qkv_width = (QUERY_HEADS + 2 * KEY_VALUE_HEADS) * HEAD_WIDTH
    hidden_units = w_down.shape[0] * dp * slots // width
    w_qkv = gather_weight(query_key_value_weight, qkv_width)
    wout = gather_weight(w_out, width)
    wgu = gather_weight(w_gate_up, 2 * hidden_units)
    wdown = gather_weight(w_down, width)
    gain_one = attn_gain.astype(F32)
    gain_two = mlp_gain.astype(F32)
    x = tokens.astype(F32)
    rms_one = lax.rsqrt(jnp.mean(x * x, axis=-1, keepdims=True) + EPS)
    normed1 = (x * rms_one * gain_one).astype(BF16)
    projected = jnp.einsum("de,scd->sec", w_qkv, normed1, preferred_element_type=F32)
    projected = projected.reshape(seqs, -1, HEAD_WIDTH, block)
    places = start + jnp.arange(block, dtype=jnp.int32)
    seg_local = lax.dynamic_slice_in_dim(segments, start, block, 1)
    position = (places[None, :] - seg_local).astype(F32)
    inverse = ROPE_BASE ** (-2.0 * jnp.arange(HEAD_WIDTH // 2, dtype=F32) / HEAD_WIDTH)
    angle = inverse[None, None, :, None] * position[:, None, None, :]
    cosine = jnp.cos(angle)
    sine = jnp.sin(angle)
    turned = rotate(projected[:, : QUERY_HEADS + KEY_VALUE_HEADS], cosine, sine).astype(BF16)
    query = turned[:, :QUERY_HEADS]
    kv_own = jnp.stack(
        [turned[:, QUERY_HEADS:], projected[:, QUERY_HEADS + KEY_VALUE_HEADS :].astype(BF16)],
        axis=1,
    )
    me_row = me.astype(jnp.int32).reshape(1)

    kv, attn_rows, lse_rows = [], [], []
    for row in range(seqs):
        own = kv_own[row]
        if row > 0:
            own, kv[-1] = lax.optimization_barrier((own, kv[-1]))
        kv.append(from_before(own, slots))
    for row in range(seqs):
        mixed, lse = attend(me_row, query[row], kv[row], seg_local[row : row + 1])
        attn_rows.append(mixed)
        lse_rows.append(lse)
    attn = jnp.stack(attn_rows).reshape(seqs, QUERY_HEADS * HEAD_WIDTH, block)

    hidden = x + jnp.einsum("sec,ed->scd", attn, wout, preferred_element_type=F32)
    rms_two = lax.rsqrt(jnp.mean(hidden * hidden, axis=-1, keepdims=True) + EPS)
    normed2 = (hidden * rms_two * gain_two).astype(BF16)
    gate_up = jnp.einsum("scd,de->sce", normed2, wgu, preferred_element_type=F32)
    gate = gate_up[..., :hidden_units]
    upper = gate_up[..., hidden_units:]
    silu_gate = jax.nn.silu(gate)
    act = (silu_gate * upper).astype(BF16)
    output = (
        hidden + jnp.einsum("scf,fd->scd", act, wdown, preferred_element_type=F32)
    ).astype(BF16)
    grad_down = jnp.einsum("scf,scd->fd", act, cotangent, preferred_element_type=F32)
    grad_down, dy = lax.optimization_barrier((grad_down.astype(BF16), cotangent))
    down_owned = scatter_sum(grad_down, dp, slots)
    d_act = jnp.einsum("scd,fd->scf", dy, wdown, preferred_element_type=F32)
    sigma = jax.nn.sigmoid(gate)
    d_gate = d_act * upper * sigma * (1.0 + gate * (1.0 - sigma))
    d_upper = d_act * silu_gate
    d_gate_up = jnp.concatenate([d_gate, d_upper], axis=-1).astype(BF16)
    grad_gate_up = jnp.einsum("scd,sce->de", normed2, d_gate_up, preferred_element_type=F32)
    grad_gate_up, d_gu = lax.optimization_barrier((grad_gate_up.astype(BF16), d_gate_up))
    gate_up_owned = scatter_sum(grad_gate_up, dp, slots)
    d_normed2 = jnp.einsum("sce,de->scd", d_gu, wgu, preferred_element_type=F32)
    d_from_norm, grad_gain_two = norm_back(hidden, rms_two, gain_two, d_normed2)
    d_hidden = cotangent.astype(F32) + d_from_norm
    d_hid_low = d_hidden.astype(BF16)
    d_attn = jnp.einsum("ed,scd->sec", wout, d_hid_low, preferred_element_type=F32).astype(BF16)
    d_attn = d_attn.reshape(seqs, QUERY_HEADS, HEAD_WIDTH, block)
    grad_out = jnp.einsum("sec,scd->ed", attn, d_hid_low, preferred_element_type=F32)
    grad_out, d_attn = lax.optimization_barrier((grad_out.astype(BF16), d_attn))
    out_owned = scatter_sum(grad_out, dp, slots)

    d_query, d_kv = [], []
    for row in range(seqs):
        d_q_row, d_kv_row = attend_back(
            me_row,
            query[row],
            kv[row],
            seg_local[row : row + 1],
            attn_rows[row],
            lse_rows[row],
            d_attn[row],
        )
        d_query.append(d_q_row)
        d_kv.append(sum_to_owner(d_kv_row, slots))
    d_query = jnp.stack(d_query)
    d_kv = jnp.stack(d_kv)
    d_turned = rotate(jnp.concatenate([d_query, d_kv[:, 0]], axis=1), cosine, -sine)
    d_proj = (
        jnp.concatenate([d_turned, d_kv[:, 1]], axis=1).reshape(seqs, -1, block).astype(BF16)
    )
    grad_qkv = jnp.einsum("scd,sec->de", normed1, d_proj, preferred_element_type=F32)
    qkv_owned = scatter_sum(grad_qkv.astype(BF16), dp, slots)
    d_normed1 = jnp.einsum("sec,de->scd", d_proj, w_qkv, preferred_element_type=F32)
    d_from_first, grad_gain_one = norm_back(x, rms_one, gain_one, d_normed1)
    input_grad = d_hidden + d_from_first
    gain_one_total, gain_two_total = lax.psum((grad_gain_one, grad_gain_two), ("dp", "seq"))
    return (
        output,
        input_grad,
        gain_one_total,
        gain_two_total,
        qkv_owned,
        out_owned,
        gate_up_owned,
        down_owned,
    )


def solution(mesh):
    rows = P("dp", "seq", None)
    flat = P(("dp", "seq"))
    return jax.shard_map(
        functools.partial(local, mesh.shape["dp"], mesh.shape["seq"]),
        mesh=mesh,
        in_specs=(rows, P("dp", None), rows, P(), P(), flat, flat, flat, flat),
        out_specs=(rows, rows, P(), P(), flat, flat, flat, flat),
        check_vma=False,
    )
```

time: 1460 us -> 903 us (0.62)
  matrix products: 405 us -> 119 us
  other arithmetic: 221 us -> 40.6 us
  waiting for transfers between devices: 669 us -> 530 us
  Pallas kernels: 0 us -> 49.1 us
  local copies, waits for them, and re-layouts: 97.9 us -> 68.2 us
  starting transfers between devices: 0.54 us -> 26.1 us
    unnamed x10 -> x13, waiting for transfers between devices: 511 us -> 34 us
    dot_general x18 -> x12, matrix products: 405 us -> 119 us  [the longest x1 19.1 us: local(): jnp.einsum('scd,de->sce', normed2, wgu, preferred_element_type=F32)]
    reduce_scatter x2 -> x7, waiting for transfers between devices: 0.02 us -> 169 us  [the longest x3 140 us: scatter_sum(): part = lax.psum_scatter(grad, 'dp', scatter_dimension=0, tiled=True)]
    ppermute x0 -> x12, waiting for transfers between devices: none -> 156 us  [the longest x6 117 us: sum_to_owner(): total += lax.ppermute(parts[slot], 'seq', pairs).astype(F32)]
    convert_element_type x5 -> x4, other arithmetic: 99.8 us -> 10.4 us  [the longest x1 9.02 us: local(): act = (silu_gate * upper).astype(BF16)]
    all_gather x2 -> x0, other arithmetic: 58 us -> none  [the longest x1 39.5 us: local(): lax.all_gather(w_out, ('dp', 'seq'), axis=0, tiled=True)]
    reshape x8 -> x4, local copies, waits for them, and re-layouts: 61.2 us -> 7.23 us  [the longest x3 6.4 us: scatter_sum(): part = part.reshape(seq, rows // dp // seq, width)]
    pallas_call x0 -> x4, Pallas kernels: none -> 49.1 us  [the longest x2 29.7 us: attend_back(): pl.pallas_call(functools.partial(attend_back_kernel, block, tile, q_tile,...]
  transfers between devices with their start and end apart: 9 -> 24, of which waited for: 6 -> 16; matrix products, arithmetic and copies ran while one was open for 27% -> 16% of each run, Pallas kernels for 0% -> 4%
where the time goes in v1:
time: 903 us; the launch traced here: 894 us
  waiting for transfers between devices  530 us (59%)
  matrix products  119 us (13%)
  local copies, waits for them, and re-layouts  68.2 us (8%)
  Pallas kernels  49.1 us (5%)
  other arithmetic  40.6 us (4%)
  blocking collectives  39.9 us (4%)
  starting transfers between devices  26.1 us (3%)
  between operations  20.6 us (2%)
    all_gather x4, waiting for transfers between devices, gather_weight(): lax.all_gather(flat.reshape(-1, width), ('dp', 'seq'), axis=0, tiled=True)  172 us
    reduce_scatter x3, waiting for transfers between devices, scatter_sum(): part = lax.psum_scatter(grad, 'dp', scatter_dimension=0, tiled=True)  140 us
    ppermute x6, waiting for transfers between devices, sum_to_owner(): total += lax.ppermute(parts[slot], 'seq', pairs).astype(F32)  117 us
    unnamed x90, local copies, waits for them, and re-layouts  48.9 us
    psum x1, blocking collectives, local(): lax.psum((grad_gain_one, grad_gain_two), ('dp', 'seq'))  39.9 us
    ppermute x6, waiting for transfers between devices, from_before(): held.append(lax.ppermute(own, 'seq', pairs))  38.3 us
    unnamed x13, waiting for transfers between devices  34 us
    pallas_call x2, Pallas kernels, attend_back(): pl.pallas_call(functools.partial(attend_back_kernel, block, tile, q_tile,...  29.7 us
  transfers between devices with their start and end apart: 24, of which 16 were waited for; matrix products, arithmetic and copies ran while one was open for 16% of the time, Pallas kernels for 4%

profile of v1, /device:TPU:0, one launch (start us, length us, event | category | flops | bytes accessed | tf_op | source)
XLA Modules:
  0.0 894.0 jit_solution(11077421189946249208)
XLA Ops:
  17.2 56.8 %all-gather.10.cloned.1.call-done = bf16[32,30,1600]{2,1,0:T(8,128)(2,1)} async-done(((bf16[1,30,1600]{2,1,0:T(8,128)(2,1)}), bf16[32,30,1600]{2,1,0:T(8,128)(2,1)}) %all-gather.10.cloned.1.call-update) | async-done | bytes 3072016 | tf_op jit(solution)/shard_map/all_gather | solution.py:47
  78.9 5.8 fusion.43
  104.7 54.4 %all-gather.12.cloned.1.call-done = bf16[32,30,960]{2,1,0:T(8,128)(2,1)} async-done(((bf16[1,30,960]{2,1,0:T(8,128)(2,1)}), bf16[32,30,960]{2,1,0:T(8,128)(2,1)}) %all-gather.12.cloned.1.call-update) | async-done | bytes 1843216 | tf_op jit(solution)/shard_map/all_gather | solution.py:47
  178.1 9.8 %attend.2 = (bf16[15,64,512]{2,1,0:T(8,128)(2,1)S(1)}, f32[15,1,512]{2,1,0:T(1,128)S(1)}) custom-call(s32[1]{0:T(128)} %bitcast.me_ref, s32[1]{0:T(128)S(6)} %select_n.14.low_ref, bf16[15,64,512]{2,1,0:T(8,128)(2,1)S(1)} %get-tuple-element.58.q_ref, bf16[4,2,5,64,512]{4,3,2,1,0:T(8,128)(2,1)S(1)} %pad_maximum_fusion.3.kv_ref, ...), custom_call_target="tpu_custom_call" | custom-call | flops 16106127360 | bytes 8388608 | tf_op jit(solution)/shard_map/attend/pallas_call | solution.py:178
  193.5 14.0 %collective-permute-done.4 = bf16[2,5,64,512]{3,2,1,0:T(8,128)(2,1)S(1)} collective-permute-done((bf16[2,5,64,512]{3,2,1,0:T(8,128)(2,1)S(1)}, bf16[2,5,64,512]{3,2,1,0:T(8,128)(2,1)S(1)}, u32[]{:S(2)}, u32[]{:S(2)}) %collective-permute-start.4) | collective-permute-done | bytes 655392 | tf_op jit(solution)/shard_map/ppermute | solution.py:229
  207.5 18.8 %collective-permute-done.3 = bf16[2,5,64,512]{3,2,1,0:T(8,128)(2,1)S(1)} collective-permute-done((bf16[2,5,64,512]{3,2,1,0:T(8,128)(2,1)S(1)}, bf16[2,5,64,512]{3,2,1,0:T(8,128)(2,1)S(1)}, u32[]{:S(2)}, u32[]{:S(2)}) %collective-permute-start.3) | collective-permute-done | bytes 655392 | tf_op jit(solution)/shard_map/ppermute | solution.py:229
  226.6 9.6 %attend.3 = (bf16[15,64,512]{2,1,0:T(8,128)(2,1)S(1)}, f32[15,1,512]{2,1,0:T(1,128)S(1)}) custom-call(s32[1]{0:T(128)} %bitcast.me_ref, s32[1]{0:T(128)S(6)} %select_n.15.low_ref, bf16[15,64,512]{2,1,0:T(8,128)(2,1)S(1)} %get-tuple-element.59.q_ref, bf16[4,2,5,64,512]{4,3,2,1,0:T(8,128)(2,1)S(1)} %pad_maximum_fusion.4.kv_ref, ...), custom_call_target="tpu_custom_call" | custom-call | flops 16106127360 | bytes 8388608 | tf_op jit(solution)/shard_map/attend/pallas_call | solution.py:178
  240.7 40.7 %all-gather.14.cloned.1.call-done = bf16[32,30,5120]{2,1,0:T(8,128)(2,1)} async-done(((bf16[1,30,5120]{2,1,0:T(8,128)(2,1)}), bf16[32,30,5120]{2,1,0:T(8,128)(2,1)}) %all-gather.14.cloned.1.call-update) | async-done | bytes 9830416 | tf_op jit(solution)/shard_map/all_gather | solution.py:47
  281.5 10.9 %reshape.160 = bf16[960,5120,1]{1,0,2:T(8,128)(2,1)} reshape(bf16[32,30,5120]{2,1,0:T(8,128)(2,1)} %all-gather.14.cloned.1.call-done) | data formatting | bytes 19660800
  292.4 19.1 %fusion.48 = f32[2,512,5120]{2,1,0:T(8,128)} fusion(bf16[960,5120,1]{1,0,2:T(8,128)(2,1)} %reshape.160, f32[2,512,960]{1,2,0:T(8,128)} %get-tuple-element.72, f32[960]{0:T(1024)S(1)} %convert_element_type.117, f32[2,512]{1,0:T(2,128)S(1)} %add_rsqrt_fusion), kind=kOutput, calls=%fused_computation.105 | convolution fusion | flops 10069278720 | bytes 34742016 | tf_op jit(solution)/shard_map/scd,de->sce/dot_general | solution.py:311
  311.5 9.0 %multiply_convert_fusion.2 = bf16[2,512,2560]{2,1,0:T(8,128)(2,1)S(1)} fusion(f32[2,512,5120]{2,1,0:T(8,128)} %fusion.48), kind=kLoop, calls=%fused_computation.4 | loop fusion | flops 15728640 | bytes 26214400 | tf_op jit(solution)/shard_map/convert_element_type | solution.py:315
  322.8 6.9 bitcast_convert_fusion.1
  329.7 19.8 %all-gather.8.cloned.1.call-done = bf16[2560,960]{1,0:T(8,128)(2,1)} async-done(((bf16[80,960]{1,0:T(8,128)(2,1)}), bf16[2560,960]{1,0:T(8,128)(2,1)}) %all-gather.8.cloned.1.call-update) | async-done | bytes 4915216 | tf_op jit(solution)/shard_map/all_gather | solution.py:47
  349.5 18.4 %multiply_convert_fusion.1 = (bf16[2,512,2560]{2,1,0:T(8,128)(2,1)}, bf16[2,512,2560]{2,1,0:T(8,128)(2,1)}) fusion(f32[2,512,5120]{2,1,0:T(8,128)} %fusion.48, bf16[2,512,960]{1,2,0:T(8,128)(2,1)} %param.11, bf16[2560,960]{1,0:T(8,128)(2,1)} %all-gather.8.cloned.1.call-done), kind=kOutput, calls=%fused_computation.3 | convolution fusion | flops 5067243520 | bytes 38338560 | tf_op jit(solution)/shard_map/scd,fd->scf/dot_general | solution.py:322
  367.9 17.6 %bitcast_convert_fusion = bf16[960,5120]{1,0:T(8,128)(2,1)} fusion(f32[2,512,960]{1,2,0:T(8,128)} %get-tuple-element.72, f32[960]{0:T(1024)S(1)} %convert_element_type.117, f32[2,512]{1,0:T(2,128)S(1)} %add_rsqrt_fusion, bf16[2,512,2560]{2,1,0:T(8,128)(2,1)} %get-tuple-element.47, bf16[2,512,2560]{2,1,0:T(8,128)(2,1)} %get-tuple-element.46), kind=kOutput, calls=%fused_computation | convolution fusion | flops 10095165440 | bytes 24256256 | tf_op jit(solution)/shard_map/scd,sce->de/dot_general | solution.py:327
  391.4 16.5 %multiply_reduce_fusion = (f32[960]{0:T(1024)}, f32[2,512]{1,0:T(2,128)S(1)}, f32[2,512,960]{1,2,0:T(8,128)}) fusion(f32[2,512,960]{1,2,0:T(8,128)S(1)} %copy-done.24, f32[2,512]{1,0:T(2,128)S(1)} %add_rsqrt_fusion, f32[960]{0:T(1024)S(1)} %convert_element_type.117, bf16[2,512,5120]{2,1,0:T(8,128)(2,1)S(1)} %pad_maximum_fusion, ...), kind=kOutput, calls=%fused_computation.31 | convolution fusion | flops 10072225792 | bytes 28196352 | tf_op jit(solution)/shard_map/sce,de->scd/dot_general | solution.py:330
  423.1 15.0 %attend_back.3 = (f32[15,64,512]{2,1,0:T(8,128)S(1)}, bf16[4,2,5,64,512]{4,3,2,1,0:T(8,128)(2,1)S(1)}) custom-call(s32[1]{0:T(128)} %bitcast.me_ref, s32[1]{0:T(128)S(6)} %select_n.15.low_ref, bf16[15,64,512]{2,1,0:T(8,128)(2,1)S(1)} %copy-done.10, bf16[4,2,5,64,512]{4,3,2,1,0:T(8,128)(2,1)S(1)} %pad_maximum_fusion.4.kv_ref, ...), custom_call_target="tpu_custom_call" | custom-call | flops 40265318400 | bytes 16777216 | tf_op jit(solution)/shard_map/attend_back/pallas_call | solution.py:204
  444.9 14.8 %attend_back.2 = (f32[15,64,512]{2,1,0:T(8,128)S(1)}, bf16[4,2,5,64,512]{4,3,2,1,0:T(8,128)(2,1)S(1)}) custom-call(s32[1]{0:T(128)} %bitcast.me_ref, s32[1]{0:T(128)S(6)} %select_n.14.low_ref, bf16[15,64,512]{2,1,0:T(8,128)(2,1)S(1)} %copy-done.8, bf16[4,2,5,64,512]{4,3,2,1,0:T(8,128)(2,1)S(1)} %copy-done.1, s32[1,512]{1,0:T(1,128)S(1)} %copy-done.12, ...), custom_call_target="tpu_custom_call" | custom-call | flops 40265318400 | bytes 16777216 | tf_op jit(solution)/shard_map/attend_back/pallas_call | solution.py:204
  464.9 8.3 collective-permute-done.9
  474.6 34.7 %collective-permute-done.11 = bf16[2,5,64,512]{3,2,1,0:T(8,128)(2,1)} collective-permute-done((bf16[2,5,64,512]{3,2,1,0:T(8,128)(2,1)}, bf16[2,5,64,512]{3,2,1,0:T(8,128)(2,1)}, u32[]{:S(2)}, u32[]{:S(2)}) %collective-permute-start.11) | collective-permute-done | bytes 655392 | tf_op jit(solution)/shard_map/ppermute | solution.py:237
  509.3 20.2 %collective-permute-done.10 = bf16[2,5,64,512]{3,2,1,0:T(8,128)(2,1)} collective-permute-done((bf16[2,5,64,512]{3,2,1,0:T(8,128)(2,1)}, bf16[2,5,64,512]{3,2,1,0:T(8,128)(2,1)}, u32[]{:S(2)}, u32[]{:S(2)}) %collective-permute-start.10) | collective-permute-done | bytes 655392 | tf_op jit(solution)/shard_map/ppermute | solution.py:237
  531.3 31.3 %collective-permute-done.8 = bf16[2,5,64,512]{3,2,1,0:T(8,128)(2,1)} collective-permute-done((bf16[2,5,64,512]{3,2,1,0:T(8,128)(2,1)}, bf16[2,5,64,512]{3,2,1,0:T(8,128)(2,1)}, u32[]{:S(2)}, u32[]{:S(2)}) %collective-permute-start.8) | collective-permute-done | bytes 655392 | tf_op jit(solution)/shard_map/ppermute | solution.py:237
  562.6 22.7 %collective-permute-done.7 = bf16[2,5,64,512]{3,2,1,0:T(8,128)(2,1)} collective-permute-done((bf16[2,5,64,512]{3,2,1,0:T(8,128)(2,1)}, bf16[2,5,64,512]{3,2,1,0:T(8,128)(2,1)}, u32[]{:S(2)}, u32[]{:S(2)}) %collective-permute-start.7) | collective-permute-done | bytes 655392 | tf_op jit(solution)/shard_map/ppermute | solution.py:237
  598.7 8.1 copy.27
  609.5 33.1 %reduce-scatter.27.cloned.1.call-done = bf16[120,1600]{1,0:T(8,128)(2,1)} async-done(((bf16[960,1600]{1,0:T(8,128)(2,1)}), bf16[120,1600]{1,0:T(8,128)(2,1)}) %reduce-scatter.27.cloned.1.call-update) | async-done | bytes 384016
  644.5 58.0 %reduce-scatter.25.cloned.1.call-done = bf16[320,960]{1,0:T(8,128)(2,1)} async-done(((bf16[2560,960]{1,0:T(8,128)(2,1)}), bf16[320,960]{1,0:T(8,128)(2,1)}) %reduce-scatter.25.cloned.1.call-update) | async-done | bytes 614416 | tf_op jit(solution)/shard_map/reduce_scatter | solution.py:243
  702.6 82.2 %reduce-scatter.19.cloned.1.call-done = bf16[120,5120]{1,0:T(8,128)(2,1)} async-done(((bf16[960,5120]{1,0:T(8,128)(2,1)}), bf16[120,5120]{1,0:T(8,128)(2,1)}) %reduce-scatter.19.cloned.1.call-update) | async-done | bytes 1228816 | tf_op jit(solution)/shard_map/reduce_scatter | solution.py:243
  787.6 10.7 %add_convert_fusion = bf16[2,512,960]{1,2,0:T(8,128)(2,1)} fusion(f32[2,512,960]{1,2,0:T(8,128)} %get-tuple-element.72, bf16[2,512,2560]{2,1,0:T(8,128)(2,1)} %copy-done.23, bf16[2560,960]{1,0:T(8,128)(2,1)} %all-gather.8.cloned.1.call-done), kind=kOutput, calls=%fused_computation.34 | convolution fusion | flops 5035130880 | bytes 16056320 | tf_op jit(solution)/shard_map/scf,fd->scd/dot_general | solution.py:317
  798.4 5.9 fusion.15
  804.3 39.9 %all-reduce.1 = (f32[960]{0:T(1024)}, f32[960]{0:T(1024)}) all-reduce(f32[960]{0:T(1024)S(1)} %get-tuple-element.42, f32[960]{0:T(1024)S(1)} %copy-done.39), channel_id=1, replica_groups=mesh['dp'=8,'seq'=4] {'dp','seq'}, use_global_device_ids=true, to_apply=%region_5.6 | all-reduce | flops 1920 | bytes 15360 | tf_op jit(solution)/shard_map/psum | solution.py:364
  844.2 6.5 fusion.11
  855.9 28.9 %reduce-scatter.21.cloned.1.call-done = bf16[1,30,5120]{2,1,0:T(8,128)(2,1)} async-done(((bf16[4,30,5120]{2,1,0:T(8,128)(2,1)}), bf16[1,30,5120]{2,1,0:T(8,128)(2,1)}) %reduce-scatter.21.cloned.1.call-update) | async-done | bytes 307216 | tf_op jit(solution)/shard_map/reduce_scatter | solution.py:248
  (176 shorter events, 124.9 us)
Async XLA Ops:
  7.2 66.8 %all-gather.10.cloned.1.call-start = ((), (), s32[]{:S(2)}) async-start(), calls=%async_computation.15 | async-start | bytes 3514368 | tf_op jit(solution)/shard_map/all_gather | solution.py:47
  8.9 150.2 %all-gather.12.cloned.1.call-start = ((), (), s32[]{:S(2)}) async-start(), calls=%async_computation.16 | async-start | bytes 2162688 | tf_op jit(solution)/shard_map/all_gather | solution.py:47
  10.6 270.9 %all-gather.14.cloned.1.call-start = ((), (), s32[]{:S(2)}) async-start(), calls=%async_computation.17 | async-start | bytes 10813440 | tf_op jit(solution)/shard_map/all_gather | solution.py:47
  12.5 337.0 %all-gather.8.cloned.1.call-start = ((), (), s32[]{:S(2)}) async-start(), calls=%async_computation.8 | async-start | bytes 5406720 | tf_op jit(solution)/shard_map/all_gather | solution.py:47
  13.3 65.6 %copy-start.35 = (f32[960]{0:T(1024)}, f32[960]{0:T(1024)S(1)}, u32[]{:S(2)}) copy-start(f32[960]{0:T(1024)S(1)} %convert_element_type.114) | copy-start | bytes 11524
  15.9 62.9 %copy-start.20 = (bf16[2,512,960]{1,2,0:T(8,128)(2,1)S(1)}, bf16[2,512,960]{1,2,0:T(8,128)(2,1)}, u32[]{:S(2)}) copy-start(bf16[2,512,960]{1,2,0:T(8,128)(2,1)} %param.9) | copy-start | bytes 5898244
  16.0 68.7 %copy-start.37 = (f32[2,512]{1,0:T(2,128)}, f32[2,512]{1,0:T(2,128)S(1)}, u32[]{:S(2)}) copy-start(f32[2,512]{1,0:T(2,128)S(1)} %add_rsqrt_fusion.1) | copy-start | bytes 12292
  17.2 67.5 %copy-start.31 = (f32[2,32,512]{2,1,0:T(8,128)}, f32[2,32,512]{2,1,0:T(8,128)S(1)}, u32[]{:S(2)}) copy-start(f32[2,32,512]{2,1,0:T(8,128)S(1)} %get-tuple-element.70) | copy-start | bytes 393220
  86.8 80.3 %collective-permute-start.2 = (bf16[2,5,64,512]{3,2,1,0:T(8,128)(2,1)}, bf16[2,5,64,512]{3,2,1,0:T(8,128)(2,1)}, u32[]{:S(2)}, u32[]{:S(2)}) collective-permute-start(bf16[2,5,64,512]{3,2,1,0:T(8,128)(2,1)} %bitcast.10), channel_id=1, source_target_pairs={{0,3},{4,7},{8,11},{12,15},{16,19},{20,23},{24,27},{28,31}} | collective-permute-start | bytes 1966088 | tf_op jit(solution)/shard_map/ppermute | solution.py:229
  91.7 75.4 %collective-permute-start.1 = (bf16[2,5,64,512]{3,2,1,0:T(8,128)(2,1)}, bf16[2,5,64,512]{3,2,1,0:T(8,128)(2,1)}, u32[]{:S(2)}, u32[]{:S(2)}) collective-permute-start(bf16[2,5,64,512]{3,2,1,0:T(8,128)(2,1)} %bitcast.10), channel_id=1, source_target_pairs={{0,2},{1,3},{4,6},{5,7},{8,10},{9,11},{12,14},{13,15},{16,18},{17,... | collective-permute-start | bytes 1966088 | tf_op jit(solution)/shard_map/ppermute | solution.py:229
  93.9 73.2 %collective-permute-start = (bf16[2,5,64,512]{3,2,1,0:T(8,128)(2,1)}, bf16[2,5,64,512]{3,2,1,0:T(8,128)(2,1)}, u32[]{:S(2)}, u32[]{:S(2)}) collective-permute-start(bf16[2,5,64,512]{3,2,1,0:T(8,128)(2,1)} %bitcast.10), channel_id=1, source_target_pairs={{0,1},{1,2},{2,3},{4,5},{5,6},{6,7},{8,9},{9,10},{10,11},{12,13},{... | collective-permute-start | bytes 1966088 | tf_op jit(solution)/shard_map/ppermute | solution.py:229
  97.2 510.4 %reduce-scatter.15.cloned.1.call-start = ((), (), s32[]{:S(2)}) async-start(), calls=%async_computation.10 | async-start | bytes 2211840 | tf_op jit(solution)/shard_map/reduce_scatter | solution.py:243
  104.7 73.5 %copy-start.11 = (s32[1,512]{1,0:T(1,128)}, s32[1,512]{1,0:T(1,128)S(1)}, u32[]{:S(2)}) copy-start(s32[1,512]{1,0:T(1,128)S(1)} %get-tuple-element.64.seg_ref) | copy-start | bytes 6148
  167.1 59.5 %copy-start.9 = (bf16[15,64,512]{2,1,0:T(8,128)(2,1)}, bf16[15,64,512]{2,1,0:T(8,128)(2,1)S(1)}, u32[]{:S(2)}) copy-start(bf16[15,64,512]{2,1,0:T(8,128)(2,1)S(1)} %get-tuple-element.59.q_ref) | copy-start | bytes 2949124
  169.9 23.6 %collective-permute-start.5 = (bf16[2,5,64,512]{3,2,1,0:T(8,128)(2,1)S(1)}, bf16[2,5,64,512]{3,2,1,0:T(8,128)(2,1)S(1)}, u32[]{:S(2)}, u32[]{:S(2)}) collective-permute-start(bf16[2,5,64,512]{3,2,1,0:T(8,128)(2,1)S(1)} %get-tuple-element.26), channel_id=1, source_target_pairs={{0,3},{4,7},{8,11},{12,15},{16,19},{20,23},{24,27},{28,31}} | collective-permute-start | bytes 1966088 | tf_op jit(solution)/shard_map/ppermute | solution.py:229
  174.3 33.2 %collective-permute-start.4 = (bf16[2,5,64,512]{3,2,1,0:T(8,128)(2,1)S(1)}, bf16[2,5,64,512]{3,2,1,0:T(8,128)(2,1)S(1)}, u32[]{:S(2)}, u32[]{:S(2)}) collective-permute-start(bf16[2,5,64,512]{3,2,1,0:T(8,128)(2,1)S(1)} %get-tuple-element.26), channel_id=1, source_target_pairs={{0,2},{1,3},{4,6},{5,7},{8,10},{9,11},{12,14},{13,15},{16,18},{17,... | collective-permute-start | bytes 1966088 | tf_op jit(solution)/shard_map/ppermute | solution.py:229
  175.6 50.6 %collective-permute-start.3 = (bf16[2,5,64,512]{3,2,1,0:T(8,128)(2,1)S(1)}, bf16[2,5,64,512]{3,2,1,0:T(8,128)(2,1)S(1)}, u32[]{:S(2)}, u32[]{:S(2)}) collective-permute-start(bf16[2,5,64,512]{3,2,1,0:T(8,128)(2,1)S(1)} %get-tuple-element.26), channel_id=1, source_target_pairs={{0,1},{1,2},{2,3},{4,5},{5,6},{6,7},{8,9},{9,10},{10,11},{12,13},{... | collective-permute-start | bytes 1966088 | tf_op jit(solution)/shard_map/ppermute | solution.py:229
  187.9 48.3 %copy-start.13 = (bf16[15,64,512]{2,1,0:T(8,128)(2,1)}, bf16[15,64,512]{2,1,0:T(8,128)(2,1)S(1)}, u32[]{:S(2)}) copy-start(bf16[15,64,512]{2,1,0:T(8,128)(2,1)S(1)} %get-tuple-element.25.out_ref) | copy-start | bytes 2949124
  423.1 21.7 %copy-start.15 = (bf16[15,64,512]{2,1,0:T(8,128)(2,1)S(1)}, bf16[15,64,512]{2,1,0:T(8,128)(2,1)}, u32[]{:S(2)}) copy-start(bf16[15,64,512]{2,1,0:T(8,128)(2,1)} %copy-done.13) | copy-start | bytes 2949124
  440.8 32.4 %collective-permute-start.9 = (bf16[2,5,64,512]{3,2,1,0:T(8,128)(2,1)S(1)}, bf16[2,5,64,512]{3,2,1,0:T(8,128)(2,1)S(1)}, u32[]{:S(2)}, u32[]{:S(2)}) collective-permute-start(bf16[2,5,64,512]{3,2,1,0:T(8,128)(2,1)S(1)} %get-tuple-element.55), channel_id=1, source_target_pairs={{1,0},{2,1},{3,2},{5,4},{6,5},{7,6},{9,8},{10,9},{11,10},{13,12},{... | collective-permute-start | bytes 1966088 | tf_op jit(solution)/shard_map/ppermute | solution.py:237
  442.2 67.0 %collective-permute-start.11 = (bf16[2,5,64,512]{3,2,1,0:T(8,128)(2,1)}, bf16[2,5,64,512]{3,2,1,0:T(8,128)(2,1)}, u32[]{:S(2)}, u32[]{:S(2)}) collective-permute-start(bf16[2,5,64,512]{3,2,1,0:T(8,128)(2,1)} %get-tuple-element.56), channel_id=1, source_target_pairs={{3,0},{7,4},{11,8},{15,12},{19,16},{23,20},{27,24},{31,28}} | collective-permute-start | bytes 1966088 | tf_op jit(solution)/shard_map/ppermute | solution.py:237
  443.5 85.9 %collective-permute-start.10 = (bf16[2,5,64,512]{3,2,1,0:T(8,128)(2,1)}, bf16[2,5,64,512]{3,2,1,0:T(8,128)(2,1)}, u32[]{:S(2)}, u32[]{:S(2)}) collective-permute-start(bf16[2,5,64,512]{3,2,1,0:T(8,128)(2,1)} %get-tuple-element.57), channel_id=1, source_target_pairs={{2,0},{3,1},{6,4},{7,5},{10,8},{11,9},{14,12},{15,13},{18,16},{19,... | collective-permute-start | bytes 1966088 | tf_op jit(solution)/shard_map/ppermute | solution.py:237
  462.3 69.0 %collective-permute-start.6 = (bf16[2,5,64,512]{3,2,1,0:T(8,128)(2,1)}, bf16[2,5,64,512]{3,2,1,0:T(8,128)(2,1)}, u32[]{:S(2)}, u32[]{:S(2)}) collective-permute-start(bf16[2,5,64,512]{3,2,1,0:T(8,128)(2,1)} %get-tuple-element.52), channel_id=1, source_target_pairs={{1,0},{2,1},{3,2},{5,4},{6,5},{7,6},{9,8},{10,9},{11,10},{13,12},{... | collective-permute-start | bytes 1966088 | tf_op jit(solution)/shard_map/ppermute | solution.py:237
  463.6 99.0 %collective-permute-start.8 = (bf16[2,5,64,512]{3,2,1,0:T(8,128)(2,1)}, bf16[2,5,64,512]{3,2,1,0:T(8,128)(2,1)}, u32[]{:S(2)}, u32[]{:S(2)}) collective-permute-start(bf16[2,5,64,512]{3,2,1,0:T(8,128)(2,1)} %get-tuple-element.53), channel_id=1, source_target_pairs={{3,0},{7,4},{11,8},{15,12},{19,16},{23,20},{27,24},{31,28}} | collective-permute-start | bytes 1966088 | tf_op jit(solution)/shard_map/ppermute | solution.py:237
  473.2 112.1 %collective-permute-start.7 = (bf16[2,5,64,512]{3,2,1,0:T(8,128)(2,1)}, bf16[2,5,64,512]{3,2,1,0:T(8,128)(2,1)}, u32[]{:S(2)}, u32[]{:S(2)}) collective-permute-start(bf16[2,5,64,512]{3,2,1,0:T(8,128)(2,1)} %get-tuple-element.54), channel_id=1, source_target_pairs={{2,0},{3,1},{6,4},{7,5},{10,8},{11,9},{14,12},{15,13},{18,16},{19,... | collective-permute-start | bytes 1966088 | tf_op jit(solution)/shard_map/ppermute | solution.py:237
  474.5 168.0 %reduce-scatter.27.cloned.1.call-start = ((), (), s32[]{:S(2)}) async-start(), calls=%async_computation.19 | async-start | bytes 3594240
  598.6 103.9 %reduce-scatter.25.cloned.1.call-start = ((), (), s32[]{:S(2)}) async-start(), calls=%async_computation.18 | async-start | bytes 5898240 | tf_op jit(solution)/shard_map/reduce_scatter | solution.py:243
  606.8 178.1 %reduce-scatter.19.cloned.1.call-start = ((), (), s32[]{:S(2)}) async-start(), calls=%async_computation.12 | async-start | bytes 11059200 | tf_op jit(solution)/shard_map/reduce_scatter | solution.py:243
  607.5 243.2 %reduce-scatter.17.cloned.1.call-start = ((), (), s32[]{:S(2)}) async-start(), calls=%async_computation.11 | async-start | bytes 327680 | tf_op jit(solution)/shard_map/reduce_scatter | solution.py:248
  609.4 242.9 %reduce-scatter.13.cloned.1.call-start = ((), (), s32[]{:S(2)}) async-start(), calls=%async_computation.9 | async-start | bytes 532480 | tf_op jit(solution)/shard_map/reduce_scatter | solution.py:248
  644.4 209.6 %reduce-scatter.23.cloned.1.call-start = ((), (), s32[]{:S(2)}) async-start(), calls=%async_computation.14 | async-start | bytes 819200 | tf_op jit(solution)/shard_map/reduce_scatter | solution.py:248
  702.5 182.2 %reduce-scatter.21.cloned.1.call-start = ((), (), s32[]{:S(2)}) async-start(), calls=%async_computation.13 | async-start | bytes 1638400 | tf_op jit(solution)/shard_map/reduce_scatter | solution.py:248
  (33 other events, 213.6 us)
Sparse Core Ops, SparseCore 0:
  11.4 62.4 all-gather.9
  77.5 81.5 all-gather.11
  162.5 118.9 all-gather.13
  284.7 64.7 all-gather.7
  474.6 102.3 reduce-scatter.14
  598.7 43.7 reduce-scatter.26
  645.9 56.5 reduce-scatter.24
  706.5 78.2 reduce-scatter.18
  787.8 19.5 reduce-scatter.16
  810.0 19.3 reduce-scatter.12
  831.8 20.4 reduce-scatter.22
  854.6 30.1 reduce-scatter.20
